TPU v7x, 32 devices: a whole 2x2x4 slice. The times are simulated.
32 devices in a mesh: groups: 2 (over y), feat: 4 (over z), node: 4 (over x, core).
Axes of the slice: x: 2, y: 2, z: 4, core: 2. Of those that a mesh axis runs over, the one named last changes fastest.
Arguments:
- features: bfloat16 [32768, 768], P(('groups', 'node'), 'feat'), parts along dimension 0, may hold values from -6 to 6
- intra_tiles: int32 [256, 3], P(('groups', 'node')), parts along dimension 0, may hold values from 0 to 31, all different within a row
- intra_values: bfloat16 [256, 3, 128, 128], P(('groups', 'node')), parts along dimension 0, may hold values from -0.3125 to 0.3125
- cut_tiles: int32 [256, 1], P(('groups', 'node')), parts along dimension 0, may hold values from 0 to 7
- cut_values: bfloat16 [256, 1, 128, 128], P(('groups', 'node')), parts along dimension 0, may hold values from -0.5 to 0.5
- send_rows: int32 [8, 4, 256], P(('groups', 'node')), parts along dimension 0, may hold values from 0 to 4095
- halo_counts: int32 [8, 4], P('groups'), parts along dimension 0, may hold values from 0 to 256, as said below
- self_l1: bfloat16 [768, 1024], replicated, may hold values from -0.21875 to 0.21875
- neigh_l1: bfloat16 [768, 1024], replicated, may hold values from -0.21875 to 0.21875
- self_l2: bfloat16 [1024, 153], replicated, may hold values from -0.1875 to 0.1875
- neigh_l2: bfloat16 [1024, 153], replicated, may hold values from -0.1875 to 0.1875
Outputs:
- logits: bfloat16 [32768, 153], P(('groups', 'node', 'feat')), parts along dimension 0
There are 2 independent parts, one for each index of `groups`. A program takes and returns all parts, laid end to end along the dimension named above; an argument that names none is the same for every part. Nothing has to cross between parts.
Inputs may be any that keep to these rules, and one draw needn't show every extreme that they name: `halo_counts`: the diagonal is 0; in every draw some reader block receives 256 live slots from every other block.
All inputs are finite; a program needn't handle non-finite values.
Results may differ from a plain program's by a relative error of at most 0.0055.
Values may be sent and summed in bfloat16 or wider, within the bound.
A program may use at most 128 MiB of HBM per device.

v0:
```python
import jax
import jax.numpy as jnp
from jax import lax
from jax.sharding import PartitionSpec as P


def tile_sum(tiles, values, source):
    picked = jnp.take(source, tiles, axis=0)
    return jnp.einsum(
        "rkij,rkjw->riw",
        values,
        picked,
        preferred_element_type=jnp.float32,
        precision=lax.Precision.HIGHEST,
    )


def shards(
    features,
    intra_tiles,
    intra_values,
    cut_tiles,
    cut_values,
    send_rows,
    halo_counts,
    self_l1,
    neigh_l1,
    self_l2,
    neigh_l2,
):
    parts = lax.axis_size("feat")
    block_rows, slice_width = features.shape
    tile_size = intra_values.shape[-1]
    row_tiles = block_rows // tile_size
    own_rows = block_rows // parts
    slots = send_rows.shape[-1]
    classes = self_l2.shape[1]
    feat_tiles = features.reshape(row_tiles, tile_size, slice_width)
    agg1 = (
        tile_sum(intra_tiles, intra_values, feat_tiles)
        .reshape(block_rows, slice_width)
        .astype(jnp.bfloat16)
    )
    feat_rows = lax.all_to_all(
        features.reshape(parts, own_rows, slice_width),
        "feat",
        split_axis=0,
        concat_axis=2,
        tiled=True,
    )
    agg_rows = lax.all_to_all(
        agg1.reshape(parts, own_rows, slice_width), "feat", split_axis=0, concat_axis=2, tiled=True
    )
    pre = jnp.dot(feat_rows[0], self_l1, preferred_element_type=jnp.float32)
    pre = pre + jnp.dot(agg_rows[0], neigh_l1, preferred_element_type=jnp.float32)
    hidden = jax.nn.relu(pre).astype(jnp.bfloat16)[None][0]
    here = lax.axis_index("node")
    arriving = lax.dynamic_index_in_dim(halo_counts, here, axis=1, keepdims=False)
    live = jnp.arange(slots)[None, :] < arriving[:, None]
    projected = jnp.dot(hidden, neigh_l2, preferred_element_type=jnp.float32)
    block_proj = lax.all_gather(projected, "feat", axis=0, tiled=True)
    outgoing = jnp.take(block_proj, send_rows[0], axis=0)
    incoming = lax.all_to_all(outgoing, "node", split_axis=0, concat_axis=0, tiled=True)
    incoming = jnp.where(live[:, :, None], incoming, 0.0).reshape(-1, tile_size, classes)
    own_tiles = own_rows // tile_size
    first_tile = lax.axis_index("feat") * own_tiles
    my_tiles = lax.dynamic_slice_in_dim(intra_tiles, first_tile, own_tiles, 0)
    my_values = lax.dynamic_slice_in_dim(intra_values, first_tile, own_tiles, 0).astype(jnp.float32)
    my_cut_tiles = lax.dynamic_slice_in_dim(cut_tiles, first_tile, own_tiles, 0)
    my_cut_values = lax.dynamic_slice_in_dim(cut_values, first_tile, own_tiles, 0).astype(
        jnp.float32
    )
    inner = tile_sum(my_tiles, my_values, block_proj.reshape(row_tiles, tile_size, classes))
    outer = tile_sum(my_cut_tiles, my_cut_values, incoming)
    neighbour = (inner + outer).reshape(own_rows, classes)
    logits = jnp.dot(hidden, self_l2, preferred_element_type=jnp.float32) + neighbour
    return logits.astype(jnp.bfloat16)


def solution(mesh):
    placed = (
        P(("groups", "node"), "feat"),
        P(("groups", "node"), None),
        P(("groups", "node"), None, None, None),
        P(("groups", "node"), None),
        P(("groups", "node"), None, None, None),
        P(("groups", "node"), None, None),
        P("groups", None),
        P(),
        P(),
        P(),
        P(),
    )
    return jax.shard_map(
        shards,
        mesh=mesh,
        in_specs=placed,
        out_specs=P(("groups", "node", "feat"), None),
        check_vma=False,
    )
```

profile of v0, /device:TPU:1, one launch (start us, length us, event | category | flops | bytes accessed | tf_op | source)
XLA Modules:
  0.0 213.5 jit_solution(10756662597694245071)
XLA Ops:
  6.5 2.9 %copy.66 = bf16[24,4,8,1024]{3,2,0,1:T(8,128)(2,1)} copy(bf16[24,4,8,1024]{3,2,1,0:T(8,128)(2,1)} %bitcast.78) | data formatting | bytes 3145728 | tf_op jit(solution)/shard_map/reshape | solution.py:45
  9.4 5.6 %all-to-all-start = ((bf16[4,1024,192]{1,2,0:T(8,128)(2,1)}), bf16[4,1024,192]{1,2,0:T(8,128)(2,1)}, u32[]{:S(2)}, u32[]{:S(2)}) async-start(bf16[4,1024,192]{1,2,0:T(8,128)(2,1)} %bitcast.79), calls=%async_computation | async-start | bytes 3145728 | tf_op jit(solution)/shard_map/all_to_all | solution.py:44
  15.3 3.1 %copy_bitcast_fusion = bf16[32,128,192]{1,2,0:T(8,128)(2,1)} fusion(bf16[4096,192]{0,1:T(8,128)(2,1)} %param.11), kind=kLoop, calls=%fused_computation.13 | loop fusion | bytes 3145728 | tf_op jit(solution)/shard_map/reshape | solution.py:38
  18.4 4.8 %gather_fusion = bf16[96,128,192]{1,2,0:T(8,128)(2,1)} fusion(bf16[32,128,192]{1,2,0:T(8,128)(2,1)} %copy_bitcast_fusion, s32[1024]{0:T(1024)S(1)} %pad_clamp_fusion.2), kind=kCustom, calls=%fused_computation | custom fusion | bytes 9437568 | tf_op jit(solution)/shard_map/jit(_take)/gather | solution.py:8
  23.2 3.9 %fusion.8 = bf16[32,128,192]{1,2,0:T(8,128)(2,1)S(1)} fusion(bf16[32,3,128,128]{3,2,1,0:T(8,128)(2,1)S(1)} %copy-done, bf16[32,3,128,192]{2,3,1,0:T(8,128)(2,1)} %bitcast.77, pred[32,3]{1,0:T(8,128)(4,1)S(1)} %copy.43), kind=kOutput, calls=%fused_computation.15 | convolution fusion | flops 607125504 | bytes 9437280 | tf_op jit(solution)/shard_map/rkij,rkjw->riw/dot_general | solution.py:9
  27.1 2.2 %copy.46 = bf16[32,128,192]{1,0,2:T(8,128)(2,1)} copy(bf16[32,128,192]{1,2,0:T(8,128)(2,1)S(1)} %fusion.8) | data formatting | bytes 3145728 | tf_op jit(solution)/shard_map/convert_element_type | solution.py:42
  29.3 3.5 %convert_element_type.20 = bf16[4,1024,192]{1,0,2:T(4,128)(2,1)} reshape(bf16[32,128,192]{1,0,2:T(8,128)(2,1)} %copy.46) | data formatting | bytes 3145728 | tf_op jit(solution)/shard_map/convert_element_type | solution.py:42
  32.8 3.1 %copy.47 = bf16[4,1024,192]{1,2,0:T(8,128)(2,1)} copy(bf16[4,1024,192]{1,0,2:T(4,128)(2,1)} %convert_element_type.20) | data formatting | bytes 3145728 | tf_op jit(solution)/shard_map/convert_element_type | solution.py:42
  35.9 15.6 %all-to-all-done = bf16[4,1024,192]{1,2,0:T(8,128)(2,1)} async-done(((bf16[4,1024,192]{1,2,0:T(8,128)(2,1)}), bf16[4,1024,192]{1,2,0:T(8,128)(2,1)}, u32[]{:S(2)}, u32[]{:S(2)}) %all-to-all-start) | async-done | bytes 1572896 | tf_op jit(solution)/shard_map/all_to_all | solution.py:44
  51.5 4.4 %all-to-all-start.1 = ((bf16[4,1024,192]{1,2,0:T(8,128)(2,1)}), bf16[4,1024,192]{1,2,0:T(8,128)(2,1)}, u32[]{:S(2)}, u32[]{:S(2)}) async-start(bf16[4,1024,192]{1,2,0:T(8,128)(2,1)} %copy.47), calls=%async_computation.1 | async-start | bytes 3145728 | tf_op jit(solution)/shard_map/all_to_all | solution.py:51
  56.0 5.7 %fusion.29 = f32[1024,1024]{1,0:T(8,128)} fusion(bf16[1024,768]{0,1:T(8,128)(2,1)} %bitcast.2, bf16[768,1024]{1,0:T(8,128)(2,1)} %param.18), kind=kOutput, calls=%fused_computation.53 | convolution fusion | flops 1610612736 | bytes 7340032 | tf_op jit(solution)/shard_map/dot_general | solution.py:54
  61.6 30.8 %all-to-all-done.1 = bf16[4,1024,192]{1,2,0:T(8,128)(2,1)} async-done(((bf16[4,1024,192]{1,2,0:T(8,128)(2,1)}), bf16[4,1024,192]{1,2,0:T(8,128)(2,1)}, u32[]{:S(2)}, u32[]{:S(2)}) %all-to-all-start.1) | async-done | bytes 1572896 | tf_op jit(solution)/shard_map/all_to_all | solution.py:51
  92.4 5.0 %maximum_convert_fusion = bf16[1024,1024]{1,0:T(8,128)(2,1)S(1)} fusion(f32[1024,1024]{1,0:T(8,128)} %fusion.29, bf16[1024,768]{0,1:T(8,128)(2,1)} %bitcast.9, bf16[768,1024]{1,0:T(8,128)(2,1)} %param.19), kind=kOutput, calls=%fused_computation.7 | convolution fusion | flops 1613758464 | bytes 9437184 | tf_op jit(solution)/shard_map/dot_general | solution.py:55
  101.2 54.1 %all-gather.2.cloned.1.call-done = f32[4096,153]{0,1:T(8,128)} async-done(((f32[1024,153]{0,1:T(8,128)}), f32[4096,153]{0,1:T(8,128)}) %all-gather.2.cloned.1.call-update) | async-done | bytes 2506768 | tf_op jit(solution)/shard_map/all_gather | solution.py:61
  155.3 3.7 %copy.60 = f32[20,8,32,128]{3,2,1,0:T(8,128)} copy(f32[20,8,32,128]{3,1,2,0:T(8,128)} %bitcast.75) | data formatting | bytes 5242880
  159.0 4.9 %copy.51 = f32[4096,153]{1,0:T(8,128)} copy(f32[4096,153]{0,1:T(8,128)} %all-gather.2.cloned.1.call-done) | data formatting | bytes 5013504 | tf_op jit(solution)/shard_map/all_gather | solution.py:61
  163.9 6.9 %gather_fusion.2 = f32[1024,153]{1,0:T(8,128)} fusion(f32[4096,153]{1,0:T(8,128)} %copy.51, s32[1024]{0:T(1024)S(1)} %broadcast_clamp_fusion), kind=kCustom, calls=%fused_computation.2 | custom fusion | bytes 1257472 | tf_op jit(solution)/shard_map/jit(_take)/gather | solution.py:62
  170.8 2.4 %copy.52 = f32[4,256,153]{1,2,0:T(8,128)} copy(f32[4,256,153]{2,1,0:T(8,128)} %bitcast.81) | data formatting | bytes 1253376 | tf_op jit(solution)/shard_map/jit(_take)/gather | solution.py:62
  175.3 4.8 %all-to-all-start.2 = ((f32[4,256,153]{1,2,0:T(8,128)}), f32[4,256,153]{1,2,0:T(8,128)}, u32[]{:S(2)}, u32[]{:S(2)}) async-start(f32[4,256,153]{1,2,0:T(8,128)} %broadcast_select_fusion.1), calls=%async_computation.2 | async-start | bytes 1310720 | tf_op jit(solution)/shard_map/all_to_all | solution.py:63
  182.0 3.0 %copy.50 = f32[32,128,153]{1,2,0:T(8,128)} copy(f32[32,128,153]{1,0,2:T(8,128)S(1)} %slice_bitcast_fusion) | data formatting | bytes 5013504 | tf_op jit(solution)/shard_map/reshape | solution.py:73
  185.0 3.7 %gather_fusion.1 = f32[24,128,153]{1,2,0:T(8,128)} fusion(f32[32,128,153]{1,2,0:T(8,128)} %copy.50, s32[1024]{0:T(1024)S(1)} %pad_clamp_fusion.1), kind=kCustom, calls=%fused_computation.1 | custom fusion | bytes 3760224 | tf_op jit(solution)/shard_map/jit(_take)/gather | solution.py:8
  188.7 3.6 %fusion.11 = f32[8,128,153]{1,2,0:T(8,128)} fusion(f32[8,3,128,153]{2,3,1,0:T(8,128)} %bitcast.74, pred[8,3]{1,0:T(8,128)(4,1)S(1)} %copy.48, bf16[32,3,128,128]{3,2,1,0:T(8,128)(2,1)S(1)} %copy-done, s32[]{:T(128)S(6)} %select_n.66), kind=kOutput, calls=%fused_computation.16 | convolution fusion | flops 722414592 | bytes 3294212 | tf_op jit(solution)/shard_map/rkij,rkjw->riw/dot_general | solution.py:9
  194.7 2.2 %reshape.107 = f32[8,128,153]{1,0,2:T(8,128)} reshape(f32[4,256,153]{1,0,2:T(4,128)} %copy.53) | data formatting | bytes 1253376 | tf_op jit(solution)/shard_map/reshape | solution.py:64
  198.9 2.5 %gather_fusion.3 = f32[8,128,153]{1,2,0:T(8,128)} fusion(f32[8,128,153]{1,2,0:T(8,128)} %copy.54, s32[1024]{0:T(1024)S(1)} %pad_clamp_fusion), kind=kCustom, calls=%fused_computation.3 | custom fusion | bytes 1253408 | tf_op jit(solution)/shard_map/jit(_take)/gather | solution.py:8
  (51 shorter events, 17.7 us)
Async XLA Ops:
  6.5 16.7 %copy-start = (bf16[32,3,128,128]{3,2,1,0:T(8,128)(2,1)S(1)}, bf16[32,3,128,128]{3,2,1,0:T(8,128)(2,1)}, u32[]{:S(2)}) copy-start(bf16[32,3,128,128]{3,2,1,0:T(8,128)(2,1)} %param.13) | copy-start | bytes 9437188
  9.4 5.6 %copy-start.5 = (s32[32,3]{0,1:T(4,128)S(1)}, s32[32,3]{0,1:T(4,128)}, u32[]{:S(2)}) copy-start(s32[32,3]{0,1:T(4,128)} %param.12) | copy-start | bytes 1156
  9.4 42.1 %all-to-all-start = ((bf16[4,1024,192]{1,2,0:T(8,128)(2,1)}), bf16[4,1024,192]{1,2,0:T(8,128)(2,1)}, u32[]{:S(2)}, u32[]{:S(2)}) async-start(bf16[4,1024,192]{1,2,0:T(8,128)(2,1)} %bitcast.79), calls=%async_computation | async-start | bytes 3145728 | tf_op jit(solution)/shard_map/all_to_all | solution.py:44
  51.5 40.9 %all-to-all-start.1 = ((bf16[4,1024,192]{1,2,0:T(8,128)(2,1)}), bf16[4,1024,192]{1,2,0:T(8,128)(2,1)}, u32[]{:S(2)}, u32[]{:S(2)}) async-start(bf16[4,1024,192]{1,2,0:T(8,128)(2,1)} %copy.47), calls=%async_computation.1 | async-start | bytes 3145728 | tf_op jit(solution)/shard_map/all_to_all | solution.py:51
  55.9 99.4 %all-gather.2.cloned.1.call-start = ((), (), s32[]{:S(2)}) async-start(), calls=%async_computation.3 | async-start | bytes 3276800 | tf_op jit(solution)/shard_map/all_gather | solution.py:61
  92.4 6.4 %copy-start.4 = (bf16[1024,153]{0,1:T(8,128)(2,1)S(1)}, bf16[1024,153]{0,1:T(8,128)(2,1)}, u32[]{:S(2)}) copy-start(bf16[1024,153]{0,1:T(8,128)(2,1)} %param.21) | copy-start | bytes 940036
  97.4 1.3 copy-start.1
  98.8 2.1 copy-start.6
  98.8 2.1 copy-start.7
  98.8 2.3 %copy-start.8 = (s32[32,1]{0,1:T(1,128)S(1)}, s32[32,1]{0,1:T(1,128)}, u32[]{:S(2)}) copy-start(s32[32,1]{0,1:T(1,128)} %param.14) | copy-start | bytes 388
  175.3 17.0 %all-to-all-start.2 = ((f32[4,256,153]{1,2,0:T(8,128)}), f32[4,256,153]{1,2,0:T(8,128)}, u32[]{:S(2)}, u32[]{:S(2)}) async-start(f32[4,256,153]{1,2,0:T(8,128)} %broadcast_select_fusion.1), calls=%async_computation.2 | async-start | bytes 1310720 | tf_op jit(solution)/shard_map/all_to_all | solution.py:63
  203.5 1.6 copy-start.2
  203.5 1.6 copy-start.3
Sparse Core Ops, SparseCore 0:
  100.6 54.6 all-gather.1
where the time goes:
time: 215 us; the launch traced here: 214 us
  waiting for transfers between devices  101 us (47%)
  local copies, waits for them, and re-layouts  57.7 us (27%)
  matrix products  23.5 us (11%)
  starting transfers between devices  14.8 us (7%)
  between operations  13.5 us (6%)
  other arithmetic  3.48 us (2%)
    all_gather x1, waiting for transfers between devices, shards(): block_proj = lax.all_gather(projected, 'feat', axis=0, tiled=True)  54.1 us
    all_to_all x1, waiting for transfers between devices, shards(): lax.all_to_all(agg1.reshape(parts, own_rows, slice_width), 'feat', split_...  30.8 us
    all_to_all x1, waiting for transfers between devices, shards(): lax.all_to_all(features.reshape(parts, own_rows, slice_width), 'feat', sp...  15.6 us
    gather x3, local copies, waits for them, and re-layouts, tile_sum(): picked = jnp.take(source, tiles, axis=0)  11.1 us
    dot_general x3, matrix products, tile_sum(): jnp.einsum('rkij,rkjw->riw', values, picked, preferred_element_type=jnp.f...  9.57 us
    gather x2, local copies, waits for them, and re-layouts, shards(): outgoing = jnp.take(block_proj, send_rows[0], axis=0)  9.29 us
    convert_element_type x3, local copies, waits for them, and re-layouts, shards(): agg1 = tile_sum(intra_tiles, intra_values, feat_tiles).reshape(block_rows...  8.78 us
    unnamed x22, local copies, waits for them, and re-layouts  6.26 us
  transfers between devices with their start and end apart: 4, of which 3 were waited for; matrix products, arithmetic and copies ran while one was open for 19% of the time, Pallas kernels for 0%

commit v1 on v0

--- a/solution.py
+++ b/solution.py
@@ -1,7 +1,368 @@
 import jax
 import jax.numpy as jnp
 from jax import lax
+from jax.experimental import pallas as pl
+from jax.experimental.pallas import tpu as pltpu
 from jax.sharding import PartitionSpec as P
+
+MESH = pl.DeviceIdType.MESH
+CHUNKS = 2
+
+
+def pack(x, lanes):
+    groups = 128 // lanes
+    height = x.shape[0] // groups
+    tail = x[:, 128 : 128 + lanes]
+    folded = jnp.concatenate([tail[q * height : (q + 1) * height] for q in range(groups)], axis=1)
+    return jnp.concatenate([x[:, :128], folded], axis=0)
+
+
+def unfold(folded, lanes):
+    groups = 128 // lanes
+    return jnp.concatenate(
+        [folded[:, q * lanes : (q + 1) * lanes] for q in range(groups)], axis=0
+    )
+
+
+def kernel(
+    intra_t, cut_t, send_rows,
+    feats_h, vals_h, cvals_h, w1s_h, w1n_h, w2_h,
+    out_ref,
+    feats, vals, cvals, w1, w2, pk, rv, acc, hid, own, gath, flat, blocks, hrows, hsend, hrecv, hflat,
+    lsem, s1, r1, s2, r2, s3, r3,
+):
+    z, n = lax.axis_index("feat"), lax.axis_index("node")
+    nz, nn = lax.axis_size("feat"), lax.axis_size("node")
+    tiles, ts, width = feats.shape
+    rest = width - 128
+    own_tiles = tiles // nz
+    ct = own_tiles // CHUNKS
+    intra_k = vals.shape[1]
+    slots = send_rows.shape[-1]
+    htiles = slots // ts
+    classes = out_ref.shape[-1]
+    f32, bf16 = jnp.float32, jnp.bfloat16
+
+    local = [
+        pltpu.make_async_copy(feats_h, feats, lsem.at[0]),
+        pltpu.make_async_copy(vals_h, vals, lsem.at[1]),
+        pltpu.make_async_copy(w1s_h, w1.at[0], lsem.at[2]),
+        pltpu.make_async_copy(w1n_h, w1.at[1], lsem.at[3]),
+        pltpu.make_async_copy(w2_h, w2, lsem.at[4]),
+        pltpu.make_async_copy(cvals_h, cvals, lsem.at[5]),
+    ]
+    for copy in local:
+        copy.start()
+
+    barrier = pltpu.get_barrier_semaphore()
+    for off in range(1, nz):
+        pl.semaphore_signal(barrier, inc=1, device_id={"feat": lax.rem(z + off, nz)}, device_id_type=MESH)
+    for off in range(1, nn):
+        pl.semaphore_signal(barrier, inc=1, device_id={"node": lax.rem(n + off, nn)}, device_id_type=MESH)
+    local[0].wait()
+
+    def pack_feats(t):
+        pk[0, t] = pack(feats[t].astype(f32), rest).astype(bf16)
+
+    def pack_agg(t):
+        picked = jnp.concatenate([feats[intra_t[t, k]] for k in range(intra_k)], axis=0)
+        weights = jnp.concatenate([vals[t, k] for k in range(intra_k)], axis=1)
+        total = jnp.dot(weights, picked, preferred_element_type=f32)
+        pk[1, t] = pack(total, rest).astype(bf16)
+
+    def l1_copy(kind, off, c):
+        to = lax.rem(z + off, nz)
+        return pltpu.make_async_remote_copy(
+            src_ref=pk.at[kind, pl.ds(to * own_tiles + c * ct, ct)],
+            dst_ref=rv.at[kind, z, pl.ds(c * ct, ct)],
+            send_sem=s1.at[kind, off - 1, c],
+            recv_sem=r1.at[kind, off - 1, c],
+            device_id={"feat": to},
+            device_id_type=MESH,
+        )
+
+    order = [2, 1, 3] if nz == 4 else list(range(1, nz))
+    for c in range(CHUNKS):
+        for kind in range(2):
+            if c == 0 and kind == 1:
+                local[1].wait()
+            for off in order + [0]:
+                to = lax.rem(z + off, nz)
+                base = to * own_tiles + c * ct
+
+                def step(i, _, kind=kind, base=base):
+                    (pack_feats if kind == 0 else pack_agg)(base + i)
+                    return 0
+
+                lax.fori_loop(0, ct, step, 0)
+                if off == 0:
+                    rv[kind, z, c * ct : (c + 1) * ct] = pk[kind, pl.ds(base, ct)]
+                else:
+                    if c == 0 and kind == 0 and off == order[0]:
+                        pl.semaphore_wait(barrier, nz - 1 + nn - 1)
+                    l1_copy(kind, off, c).start()
+    for copy in local[2:]:
+        copy.wait()
+
+    def accumulate(kind, source, c, first=False):
+        rows = []
+        for i in range(ct):
+            record = rv[kind, source, c * ct + i]
+            tail = unfold(record[ts:].astype(f32), rest).astype(bf16)
+            rows.append(jnp.concatenate([record[:ts], tail], axis=1))
+        lhs = jnp.concatenate(rows, axis=0)
+        part = jnp.dot(lhs, w1[kind, source], preferred_element_type=f32)
+        if first:
+            acc[...] = part
+        else:
+            acc[...] += part
+
+    def from_others(kind, c):
+        def step(off, _):
+            l1_copy(kind, off, c).wait_recv()
+            accumulate(kind, lax.rem(z + nz - off, nz), c)
+            return 0
+
+        lax.fori_loop(1, nz, step, 0)
+
+    def ag_copy(c, right, k):
+        source = z - k if right else z + k
+        piece = gath.at[pl.ds(source * own_tiles + c * ct, ct)]
+        side = 1 if right else 0
+        return pltpu.make_async_remote_copy(
+            src_ref=piece,
+            dst_ref=piece,
+            send_sem=s2.at[c, side, k],
+            recv_sem=r2.at[c, side, k],
+            device_id={"feat": z + 1 if right else z - 1},
+            device_id_type=MESH,
+        )
+
+    def ag_send(c, k):
+        @pl.when((z - k >= 0) & (z + 1 < nz))
+        def _():
+            ag_copy(c, True, k).start()
+
+        @pl.when((z + k < nz) & (z >= 1))
+        def _():
+            ag_copy(c, False, k).start()
+
+    def ag_sent(c, k):
+        @pl.when((z - k >= 0) & (z + 1 < nz))
+        def _():
+            ag_copy(c, True, k).wait_send()
+
+        @pl.when((z + k < nz) & (z >= 1))
+        def _():
+            ag_copy(c, False, k).wait_send()
+
+    def flatten(source, c):
+        def step(i, _):
+            t = source * own_tiles + c * ct + i
+            record = gath[t]
+            tail = unfold(record[ts:].astype(f32), 32)
+            rows = pl.ds(pl.multiple_of(t * ts, ts), ts)
+            flat[rows, :128] = record[:ts].astype(f32)
+            flat[rows, 128:160] = tail
+            blocks[t, :, :128] = record[:ts]
+            blocks[t, :, 128:160] = tail.astype(bf16)
+            return 0
+
+        lax.fori_loop(0, ct, step, 0)
+
+    def ag_step(c, k):
+        def arrived(right, source):
+            piece = gath.at[pl.ds(source * own_tiles + c * ct, ct)]
+            side = 1 if right else 0
+            pltpu.make_async_copy(piece, piece, r2.at[c, side, k - 1]).wait()
+
+        @pl.when(z - k >= 0)
+        def _():
+            arrived(True, z - k)
+
+            @pl.when(z + 1 < nz)
+            def _():
+                if k < nz - 1:
+                    ag_copy(c, True, k).start()
+
+        @pl.when(z + k < nz)
+        def _():
+            arrived(False, z + k)
+
+            @pl.when(z >= 1)
+            def _():
+                if k < nz - 1:
+                    ag_copy(c, False, k).start()
+
+        @pl.when(z - k >= 0)
+        def _():
+            flatten(z - k, c)
+
+        @pl.when(z + k < nz)
+        def _():
+            flatten(z + k, c)
+
+    flat[:, 128:] = jnp.zeros((flat.shape[0], 128), f32)
+    flat[tiles * ts :, :128] = jnp.zeros((8, 128), f32)
+    blocks[:, :, 128:] = jnp.zeros((tiles, ts, 128), bf16)
+
+    def project(c):
+        hid[...] = jnp.maximum(acc[...], 0.0).astype(bf16)
+        both = jnp.dot(hid[...], w2[...], preferred_element_type=f32)
+        own[c * ct * ts : (c + 1) * ct * ts, :] = both[:, 256:]
+        for i in range(ct):
+            gath[z * own_tiles + c * ct + i] = pack(
+                both[i * ts : (i + 1) * ts, :256], 32
+            ).astype(bf16)
+        ag_send(c, 0)
+        flatten(z, c)
+
+    for c in range(CHUNKS):
+        accumulate(0, z, c, first=True)
+        accumulate(1, z, c)
+        from_others(0, c)
+        if c > 0:
+            ag_step(c - 1, 1)
+        from_others(1, c)
+        project(c)
+        if c > 0:
+            for k in range(2, nz):
+                ag_step(c - 1, k)
+    for k in range(1, nz):
+        ag_step(CHUNKS - 1, k)
+
+    def h_copy(off):
+        to = lax.rem(n + off, nn)
+        return pltpu.make_async_remote_copy(
+            src_ref=hsend.at[off - 1],
+            dst_ref=hrecv.at[n],
+            send_sem=s3.at[off - 1],
+            recv_sem=r3.at[off - 1],
+            device_id={"node": to},
+            device_id_type=MESH,
+        )
+
+    for off in range(1, nn):
+        to = lax.rem(n + off, nn)
+
+        def pick(i, _, to=to):
+            for u in range(16):
+                j = i * 16 + u
+                hrows[j] = flat[send_rows[0, to, j]]
+            return 0
+
+        lax.fori_loop(0, slots // 16, pick, 0)
+        for h in range(htiles):
+            hsend[off - 1, h] = pack(hrows[h * ts : (h + 1) * ts, :], 32).astype(bf16)
+        h_copy(off).start()
+
+    hflat[...] = jnp.zeros_like(hflat)
+
+    def inner(i, _):
+        t = z * own_tiles + i
+        picked = jnp.concatenate(
+            [blocks[intra_t[t, k]] for k in range(intra_k)], axis=0
+        )
+        weights = jnp.concatenate([vals[t, k] for k in range(intra_k)], axis=1)
+        rows = pl.ds(pl.multiple_of(i * ts, ts), ts)
+        own[rows, :] += jnp.dot(weights, picked, preferred_element_type=f32)
+        return 0
+
+    lax.fori_loop(0, own_tiles, inner, 0)
+
+    for off in range(1, nn):
+        h_copy(off).wait_recv()
+        source = lax.rem(n + nn - off, nn)
+        for h in range(htiles):
+            record = hrecv[source, h]
+            t = source * htiles + h
+            hflat[t, :, :128] = record[:ts]
+            hflat[t, :, 128:160] = unfold(record[ts:].astype(f32), 32).astype(bf16)
+
+    def outer(i, _):
+        t = z * own_tiles + i
+        rows = pl.ds(pl.multiple_of(i * ts, ts), ts)
+        total = own[rows, :]
+        for k in range(cvals.shape[1]):
+            total += jnp.dot(cvals[t, k], hflat[cut_t[t, k]], preferred_element_type=f32)
+        out_ref[rows, :] = total[:, :classes].astype(bf16)
+        return 0
+
+    lax.fori_loop(0, own_tiles, outer, 0)
+
+    for c in range(CHUNKS):
+        for kind in range(2):
+            for off in range(1, nz):
+                l1_copy(kind, off, c).wait_send()
+        for k in range(nz - 1):
+            ag_sent(c, k)
+    for off in range(1, nn):
+        h_copy(off).wait_send()
+
+
+def fused(
+    features, intra_tiles, intra_values, cut_tiles, cut_values, send_rows, halo_counts,
+    self_l1, neigh_l1, self_l2, neigh_l2,
+):
+    nz, nn = lax.axis_size("feat"), lax.axis_size("node")
+    block_rows, width = features.shape
+    ts = intra_values.shape[-1]
+    tiles = block_rows // ts
+    own_rows = block_rows // nz
+    own_tiles = tiles // nz
+    hidden = self_l1.shape[1]
+    classes = self_l2.shape[1]
+    slots = send_rows.shape[-1]
+    htiles = slots // ts
+    pad = ((0, 0), (0, 256 - classes))
+    w2 = jnp.concatenate([jnp.pad(neigh_l2, pad), jnp.pad(self_l2, pad)], axis=1)
+    leaving = halo_counts[lax.axis_index("node")]
+    rows = jnp.where(jnp.arange(slots)[None, None, :] < leaving[None, :, None], send_rows, block_rows)
+    record = ts + ts * (width - 128) // 128
+    ct = own_tiles // CHUNKS
+    bf16, f32 = jnp.bfloat16, jnp.float32
+    smem = pl.BlockSpec(memory_space=pltpu.SMEM)
+    hbm = pl.BlockSpec(memory_space=pl.ANY)
+    dma = pltpu.SemaphoreType.DMA
+    return pl.pallas_call(
+        kernel,
+        out_shape=jax.ShapeDtypeStruct((own_rows, classes), bf16),
+        in_specs=[smem] * 3 + [hbm] * 6,
+        out_specs=pl.BlockSpec(memory_space=pltpu.VMEM),
+        scratch_shapes=[
+            pltpu.VMEM((tiles, ts, width), bf16),
+            pltpu.VMEM(intra_values.shape, bf16),
+            pltpu.VMEM(cut_values.shape, bf16),
+            pltpu.VMEM((2, nz, width, hidden), bf16),
+            pltpu.VMEM((hidden, 512), bf16),
+            pltpu.VMEM((2, tiles, record, 128), bf16),
+            pltpu.VMEM((2, nz, own_tiles, record, 128), bf16),
+            pltpu.VMEM((ct * ts, hidden), f32),
+            pltpu.VMEM((ct * ts, hidden), bf16),
+            pltpu.VMEM((own_rows, 256), f32),
+            pltpu.VMEM((tiles, ts + ts // 4, 128), bf16),
+            pltpu.VMEM((block_rows + 8, 256), f32),
+            pltpu.VMEM((tiles, ts, 256), bf16),
+            pltpu.VMEM((slots, 256), f32),
+            pltpu.VMEM((nn - 1, htiles, ts + ts // 4, 128), bf16),
+            pltpu.VMEM((nn, htiles, ts + ts // 4, 128), bf16),
+            pltpu.VMEM((nn * htiles, ts, 256), bf16),
+            dma((6,)),
+            dma((2, nz - 1, CHUNKS)),
+            dma((2, nz - 1, CHUNKS)),
+            dma((CHUNKS, 2, nz - 1)),
+            dma((CHUNKS, 2, nz - 1)),
+            dma((nn - 1,)),
+            dma((nn - 1,)),
+        ],
+        compiler_params=pltpu.CompilerParams(
+            collective_id=0, has_side_effects=True, vmem_limit_bytes=56 * 1024 * 1024
+        ),
+    )(
+        intra_tiles, cut_tiles, rows,
+        features.reshape(tiles, ts, width), intra_values, cut_values,
+        self_l1.reshape(nz, width, hidden), neigh_l1.reshape(nz, width, hidden), w2,
+    )
 
 
 def tile_sum(tiles, values, source):
@@ -30,6 +391,11 @@
 ):
     parts = lax.axis_size("feat")
     block_rows, slice_width = features.shape
+    if slice_width == 192 and block_rows <= 4096 and 128 < self_l2.shape[1] <= 160:
+        return fused(
+            features, intra_tiles, intra_values, cut_tiles, cut_values, send_rows, halo_counts,
+            self_l1, neigh_l1, self_l2, neigh_l2,
+        )
     tile_size = intra_values.shape[-1]
     row_tiles = block_rows // tile_size
     own_rows = block_rows // parts

time: 215 us -> 121 us (0.56)
  Pallas kernels: 0 us -> 107 us
  waiting for transfers between devices: 101 us -> 0 us
  local copies, waits for them, and re-layouts: 57.7 us -> 10.1 us
  matrix products: 23.5 us -> 0 us
  starting transfers between devices: 14.8 us -> 0 us
  between operations: 13.5 us -> 0.02 us
    pallas_call x0 -> x1, Pallas kernels: none -> 107 us  [fused(): pl.pallas_call(kernel, out_shape=jax.ShapeDtypeStruct((own_rows, classes)...]
    all_gather x1 -> x0, waiting for transfers between devices: 54.1 us -> none  [shards(): block_proj = lax.all_gather(projected, 'feat', axis=0, tiled=True)]
    all_to_all x3 -> x0, waiting for transfers between devices: 46.4 us -> none  [the longest x1 30.8 us: shards(): lax.all_to_all(agg1.reshape(parts, own_rows, slice_width), 'feat', split_...]
    dot_general x7 -> x0, matrix products: 23.5 us -> none  [the longest x3 9.57 us: tile_sum(): jnp.einsum('rkij,rkjw->riw', values, picked, preferred_element_type=jnp.f...]
    gather x5 -> x0, local copies, waits for them, and re-layouts: 20.3 us -> none  [the longest x3 11.1 us: tile_sum(): picked = jnp.take(source, tiles, axis=0)]
    reshape x6 -> x0, local copies, waits for them, and re-layouts: 15 us -> none  [the longest x2 4.88 us: shards(): block_proj.reshape(row_tiles, tile_size, classes)]
    all_to_all x3 -> x0, starting transfers between devices: 14.7 us -> none  [the longest x1 5.55 us: shards(): lax.all_to_all(features.reshape(parts, own_rows, slice_width), 'feat', sp...]
    convert_element_type x3 -> x0, local copies, waits for them, and re-layouts: 8.78 us -> none  [shards(): agg1 = tile_sum(intra_tiles, intra_values, feat_tiles).reshape(block_rows...]
  transfers between devices with their start and end apart: 4 -> 0, of which waited for: 3 -> 0; matrix products, arithmetic and copies ran while one was open for 19% -> 0% of each run, Pallas kernels for 0% -> 0%
where the time goes in v1:
time: 121 us; the launch traced here: 120 us
  Pallas kernels  107 us (88%)
  local copies, waits for them, and re-layouts  10.1 us (8%)
  other arithmetic  2.51 us (2%)
    pallas_call x1, Pallas kernels, fused(): pl.pallas_call(kernel, out_shape=jax.ShapeDtypeStruct((own_rows, classes)...  107 us
    unnamed x9, local copies, waits for them, and re-layouts  8.18 us

profile of v1, /device:TPU:1, one launch (start us, length us, event | category | flops | bytes accessed | tf_op | source)
XLA Modules:
  0.0 120.2 jit_solution(16125854392037190553)
XLA Ops:
  0.0 0.0 copy-start
  0.0 0.0 copy-start.1
  0.0 0.7 copy-done
  0.7 1.3 %fusion.3.send_rows = s32[1,4,256]{2,1,0:T(4,128)} fusion(s32[1,4,256]{2,1,0:T(4,128)} %param.16, s32[4]{0:T(128)S(1)} %dynamic-slice_bitcast_fusion), kind=kLoop, calls=%fused_computation.6 | loop fusion | flops 2048 | bytes 8208 | tf_op jit(solution)/shard_map/jit(_where)/select_n | solution.py:320
  2.0 1.4 %copy.15.intra_t = s32[32,3]{1,0:T(8,128)} copy(s32[32,3]{0,1:T(4,128)} %param.12) | data formatting | bytes 768 | tf_op args[1]
  3.4 1.3 %copy.16.cut_t = s32[32,1]{1,0:T(8,128)} copy(s32[32,1]{0,1:T(1,128)} %param.14) | data formatting | bytes 256 | tf_op args[3]
  4.7 1.2 copy.14
  5.9 1.2 copy.13
  7.1 1.2 fusion.2.w2_h
  8.3 0.0 copy-done.1
  8.3 2.4 %copy.12 = bf16[4096,192]{1,0:T(8,128)(2,1)} copy(bf16[4096,192]{0,1:T(8,128)(2,1)S(1)} %copy-done.1) | data formatting | bytes 3145728 | tf_op args[0]
  10.7 107.5 %shard_map.109 = bf16[1024,153]{1,0:T(8,128)(2,1)} custom-call(s32[32,3]{1,0:T(8,128)} %copy.15.intra_t, s32[32,1]{1,0:T(8,128)} %copy.16.cut_t, s32[1,4,256]{2,1,0:T(4,128)} %fusion.3.send_rows, bf16[32,128,192]{2,1,0:T(8,128)(2,1)} %bitcast.5, bf16[32,3,128,128]{3,2,1,0:T(8,128)(2,1)} %vals_h.1, bf16[32,1,128,128]{3,2,1,0:T(8,128)(2,1)} %cvals_h.1, ...), custom_call_target="tpu_custom_call" | custom-call | tf_op jit(solution)/shard_map/pallas_call | solution.py:327
  118.2 1.9 %copy.17 = bf16[1024,153]{0,1:T(8,128)(2,1)} copy(bf16[1024,153]{1,0:T(8,128)(2,1)} %shard_map.109) | data formatting | bytes 626688 | tf_op jit(solution)/shard_map/pallas_call | solution.py:327
  (1 shorter events, 0.0 us)
Async XLA Ops:
  0.0 0.7 copy-start
  0.0 8.3 %copy-start.1 = (bf16[4096,192]{0,1:T(8,128)(2,1)S(1)}, bf16[4096,192]{0,1:T(8,128)(2,1)}, u32[]{:S(2)}) copy-start(bf16[4096,192]{0,1:T(8,128)(2,1)} %param.11) | copy-start | bytes 4718596

commit v2 on v1

v2 whole, which is shorter than its diff:
```python
import jax
import jax.numpy as jnp
from jax import lax
from jax.experimental import pallas as pl
from jax.experimental.pallas import tpu as pltpu
from jax.sharding import PartitionSpec as P

MESH = pl.DeviceIdType.MESH
CHUNKS = 2
F32, BF16 = jnp.float32, jnp.bfloat16


def dot(a, b, left, right):
    return lax.dot_general(a, b, (((left,), (right,)), ((), ())), preferred_element_type=F32)


def kernel(
    intra_t, cut_t, send_rows, counts,
    feats_h, vals_h, cvals_h, w1s_h, w1n_h, w2n_h, w2s_h,
    out_ref,
    whole, feats, vals, cvals, w1, w2n, w2s, agg, rv, acc, proj, own, gath, flat, hrows, hsend, hrecv,
    lsem, s1, r1, s2, r2, s3, r3,
):
    z, n = lax.axis_index("feat"), lax.axis_index("node")
    nz, nn = lax.axis_size("feat"), lax.axis_size("node")
    tiles, width, ts = feats.shape
    own_tiles = tiles // nz
    ct = own_tiles // CHUNKS
    part = ct * ts
    intra_k = vals.shape[1]
    slots = send_rows.shape[-1]
    htiles = slots // ts
    classes = out_ref.shape[0]

    local = [
        pltpu.make_async_copy(feats_h, whole, lsem.at[0]),
        pltpu.make_async_copy(vals_h, vals, lsem.at[1]),
        pltpu.make_async_copy(w1s_h, w1.at[0], lsem.at[2]),
        pltpu.make_async_copy(w1n_h, w1.at[1], lsem.at[3]),
        pltpu.make_async_copy(w2n_h, w2n, lsem.at[4]),
        pltpu.make_async_copy(w2s_h, w2s, lsem.at[5]),
        pltpu.make_async_copy(cvals_h, cvals, lsem.at[6]),
    ]
    for copy in local:
        copy.start()

    barrier = pltpu.get_barrier_semaphore()
    for off in range(1, nz):
        pl.semaphore_signal(barrier, inc=1, device_id={"feat": lax.rem(z + off, nz)}, device_id_type=MESH)
    for off in range(1, nn):
        pl.semaphore_signal(barrier, inc=1, device_id={"node": lax.rem(n + off, nn)}, device_id_type=MESH)
    local[0].wait()
    pl.semaphore_wait(barrier, nz - 1 + nn - 1)

    def l1_copy(kind, off, c):
        to = lax.rem(z + off, nz)
        if kind == 0:
            start = pl.multiple_of((to * CHUNKS + c) * part, part)
            source = whole.at[:, pl.ds(start, part)]
        else:
            source = agg.at[to, c]
        return pltpu.make_async_remote_copy(
            src_ref=source,
            dst_ref=rv.at[kind, z, c],
            send_sem=s1.at[kind, off - 1, c],
            recv_sem=r1.at[kind, off - 1, c],
            device_id={"feat": to},
            device_id_type=MESH,
        )

    order = [2, 1, 3] if nz == 4 else list(range(1, nz))
    for off in order:
        l1_copy(0, off, 0).start()
    for t in range(tiles):
        feats[t] = whole[:, t * ts : (t + 1) * ts]

    def aggregate(to, c):
        for i in range(ct):
            t = (to * CHUNKS + c) * ct + i
            picked = jnp.concatenate([feats[intra_t[k, t]] for k in range(intra_k)], axis=1)
            weights = jnp.concatenate([vals[t, k] for k in range(intra_k)], axis=1)
            agg[to, c, :, i * ts : (i + 1) * ts] = dot(picked, weights, 1, 1).astype(BF16)

    local[1].wait()
    for c in range(CHUNKS):
        if c > 0:
            for off in order:
                l1_copy(0, off, c).start()
        for off in order:
            aggregate(lax.rem(z + off, nz), c)
            l1_copy(1, off, c).start()
    for c in range(CHUNKS):
        aggregate(z, c)
    for copy in local[2:]:
        copy.wait()

    def accumulate(kind, source, block, first=False):
        term = dot(w1[kind, source], block, 0, 0)
        if first:
            acc[...] = term
        else:
            acc[...] += term

    def from_others(kind, c):
        def step(off, _):
            l1_copy(kind, off, c).wait_recv()
            source = lax.rem(z + nz - off, nz)
            accumulate(kind, source, rv[kind, source, c])
            return 0

        lax.fori_loop(1, nz, step, 0)

    def ag_piece(source, c):
        return gath.at[pl.ds(source * own_tiles + c * ct, ct)]

    def ag_copy(c, right, k):
        piece = ag_piece(z - k if right else z + k, c)
        side = 1 if right else 0
        return pltpu.make_async_remote_copy(
            src_ref=piece,
            dst_ref=piece,
            send_sem=s2.at[c, side, k],
            recv_sem=r2.at[c, side, k],
            device_id={"feat": z + 1 if right else z - 1},
            device_id_type=MESH,
        )

    def ag_send(c, k):
        @pl.when((z - k >= 0) & (z + 1 < nz))
        def _():
            ag_copy(c, True, k).start()

        @pl.when((z + k < nz) & (z >= 1))
        def _():
            ag_copy(c, False, k).start()

    def ag_sent(c, k):
        @pl.when((z - k >= 0) & (z + 1 < nz))
        def _():
            ag_copy(c, True, k).wait_send()

        @pl.when((z + k < nz) & (z >= 1))
        def _():
            ag_copy(c, False, k).wait_send()

    def flatten(source, c):
        for i in range(ct):
            t = source * own_tiles + c * ct + i
            rows = pl.ds(pl.multiple_of(t * ts, ts), ts)
            tile = gath[t].astype(F32)
            flat[rows, :128] = tile[:128].T
            flat[rows, 128:160] = tile[128:].T

    def ag_step(c, k):
        @pl.when(z - k >= 0)
        def _():
            piece = ag_piece(z - k, c)
            pltpu.make_async_copy(piece, piece, r2.at[c, 1, k - 1]).wait()
            if k < nz - 1:
                @pl.when(z + 1 < nz)
                def _():
                    ag_copy(c, True, k).start()

        @pl.when(z + k < nz)
        def _():
            piece = ag_piece(z + k, c)
            pltpu.make_async_copy(piece, piece, r2.at[c, 0, k - 1]).wait()
            if k < nz - 1:
                @pl.when(z >= 1)
                def _():
                    ag_copy(c, False, k).start()

        @pl.when(z - k >= 0)
        def _():
            flatten(z - k, c)

        @pl.when(z + k < nz)
        def _():
            flatten(z + k, c)

    proj[...] = jnp.zeros_like(proj)
    own[...] = jnp.zeros_like(own)
    flat[:, 128:] = jnp.zeros((flat.shape[0], 128), F32)

    def project(c):
        hidden = jnp.maximum(acc[...], 0.0).astype(BF16)
        proj[:classes, :] = dot(w2n[...], hidden, 1, 0)
        for i in range(ct):
            gath[z * own_tiles + c * ct + i] = proj[:, i * ts : (i + 1) * ts].astype(BF16)
        ag_send(c, 0)
        own[:classes, c * part : (c + 1) * part] = dot(w2s[...], hidden, 1, 0)
        flatten(z, c)

    for c in range(CHUNKS):
        start = pl.multiple_of((z * CHUNKS + c) * part, part)
        accumulate(0, z, whole[:, pl.ds(start, part)], first=True)
        accumulate(1, z, agg[z, c])
        from_others(0, c)
        if c > 0:
            ag_step(c - 1, 1)
        from_others(1, c)
        project(c)
        if c > 0:
            for k in range(2, nz):
                ag_step(c - 1, k)
    for k in range(1, nz):
        ag_step(CHUNKS - 1, k)

    def h_copy(off):
        return pltpu.make_async_remote_copy(
            src_ref=hsend.at[off - 1],
            dst_ref=hrecv.at[pl.ds(n * htiles, htiles)],
            send_sem=s3.at[off - 1],
            recv_sem=r3.at[off - 1],
            device_id={"node": lax.rem(n + off, nn)},
            device_id_type=MESH,
        )

    for off in range(1, nn):
        to = lax.rem(n + off, nn)

        def pick(i, _, to=to):
            for u in range(16):
                j = i * 16 + u
                hrows[j] = flat[send_rows[0, to, j]]
            return 0

        lax.fori_loop(0, slots // 16, pick, 0)
        slot = lax.broadcasted_iota(jnp.int32, (1, ts), 1)
        for h in range(htiles):
            live = jnp.clip(counts[n, to] - h * ts - slot, 0, 1).astype(F32)
            rows = hrows[h * ts : (h + 1) * ts, :].T
            hsend[off - 1, h] = (rows[:160] * live).astype(BF16)
        h_copy(off).start()
    hrecv[pl.ds(n * htiles, htiles)] = jnp.zeros((htiles,) + hrecv.shape[1:], BF16)

    for i in range(own_tiles):
        t = z * own_tiles + i
        picked = jnp.concatenate([gath[intra_t[k, t]] for k in range(intra_k)], axis=1)
        weights = jnp.concatenate([vals[t, k] for k in range(intra_k)], axis=1)
        own[:, i * ts : (i + 1) * ts] += dot(picked, weights, 1, 1)

    for off in range(1, nn):
        h_copy(off).wait_recv()
    for i in range(own_tiles):
        t = z * own_tiles + i
        total = own[:, i * ts : (i + 1) * ts]
        for k in range(cvals.shape[1]):
            total += dot(hrecv[cut_t[k, t]], cvals[t, k], 1, 1)
        out_ref[:, i * ts : (i + 1) * ts] = total[:classes].astype(BF16)

    for c in range(CHUNKS):
        for kind in range(2):
            for off in range(1, nz):
                l1_copy(kind, off, c).wait_send()
        for k in range(nz - 1):
            ag_sent(c, k)
    for off in range(1, nn):
        h_copy(off).wait_send()


def fused(
    features, intra_tiles, intra_values, cut_tiles, cut_values, send_rows, halo_counts,
    self_l1, neigh_l1, self_l2, neigh_l2,
):
    nz, nn = lax.axis_size("feat"), lax.axis_size("node")
    block_rows, width = features.shape
    ts = intra_values.shape[-1]
    tiles = block_rows // ts
    own_rows = block_rows // nz
    own_tiles = tiles // nz
    hidden = self_l1.shape[1]
    classes = self_l2.shape[1]
    slots = send_rows.shape[-1]
    htiles = slots // ts
    ct = own_tiles // CHUNKS
    part = ct * ts
    smem = pl.BlockSpec(memory_space=pltpu.SMEM)
    hbm = pl.BlockSpec(memory_space=pl.ANY)
    dma = pltpu.SemaphoreType.DMA
    vmem = pltpu.VMEM
    out = pl.pallas_call(
        kernel,
        out_shape=jax.ShapeDtypeStruct((classes, own_rows), BF16),
        in_specs=[smem] * 4 + [hbm] * 7,
        out_specs=pl.BlockSpec(memory_space=pltpu.VMEM),
        scratch_shapes=[
            vmem((width, block_rows), BF16),
            vmem((tiles, width, ts), BF16),
            vmem(intra_values.shape, BF16),
            vmem(cut_values.shape, BF16),
            vmem((2, nz, width, hidden), BF16),
            vmem((classes, hidden), BF16),
            vmem((classes, hidden), BF16),
            vmem((nz, CHUNKS, width, part), BF16),
            vmem((2, nz, CHUNKS, width, part), BF16),
            vmem((hidden, part), F32),
            vmem((160, part), F32),
            vmem((160, own_rows), F32),
            vmem((tiles, 160, ts), BF16),
            vmem((block_rows, 256), F32),
            vmem((slots, 256), F32),
            vmem((nn - 1, htiles, 160, ts), BF16),
            vmem((nn * htiles, 160, ts), BF16),
            dma((7,)),
            dma((2, nz - 1, CHUNKS)),
            dma((2, nz - 1, CHUNKS)),
            dma((CHUNKS, 2, nz - 1)),
            dma((CHUNKS, 2, nz - 1)),
            dma((nn - 1,)),
            dma((nn - 1,)),
        ],
        compiler_params=pltpu.CompilerParams(
            collective_id=0, has_side_effects=True, vmem_limit_bytes=56 * 1024 * 1024
        ),
    )(
        intra_tiles.T, cut_tiles.T, send_rows, halo_counts,
        features.T, intra_values, cut_values,
        self_l1.reshape(nz, width, hidden), neigh_l1.reshape(nz, width, hidden),
        neigh_l2.T, self_l2.T,
    )
    return out.T


def tile_sum(tiles, values, source):
    picked = jnp.take(source, tiles, axis=0)
    return jnp.einsum(
        "rkij,rkjw->riw",
        values,
        picked,
        preferred_element_type=jnp.float32,
        precision=lax.Precision.HIGHEST,
    )


def shards(
    features,
    intra_tiles,
    intra_values,
    cut_tiles,
    cut_values,
    send_rows,
    halo_counts,
    self_l1,
    neigh_l1,
    self_l2,
    neigh_l2,
):
    parts = lax.axis_size("feat")
    block_rows, slice_width = features.shape
    if slice_width == 192 and block_rows <= 4096 and 128 < self_l2.shape[1] <= 160:
        return fused(
            features, intra_tiles, intra_values, cut_tiles, cut_values, send_rows, halo_counts,
            self_l1, neigh_l1, self_l2, neigh_l2,
        )
    tile_size = intra_values.shape[-1]
    row_tiles = block_rows // tile_size
    own_rows = block_rows // parts
    slots = send_rows.shape[-1]
    classes = self_l2.shape[1]
    feat_tiles = features.reshape(row_tiles, tile_size, slice_width)
    agg1 = (
        tile_sum(intra_tiles, intra_values, feat_tiles)
        .reshape(block_rows, slice_width)
        .astype(jnp.bfloat16)
    )
    feat_rows = lax.all_to_all(
        features.reshape(parts, own_rows, slice_width),
        "feat",
        split_axis=0,
        concat_axis=2,
        tiled=True,
    )
    agg_rows = lax.all_to_all(
        agg1.reshape(parts, own_rows, slice_width), "feat", split_axis=0, concat_axis=2, tiled=True
    )
    pre = jnp.dot(feat_rows[0], self_l1, preferred_element_type=jnp.float32)
    pre = pre + jnp.dot(agg_rows[0], neigh_l1, preferred_element_type=jnp.float32)
    hidden = jax.nn.relu(pre).astype(jnp.bfloat16)[None][0]
    here = lax.axis_index("node")
    arriving = lax.dynamic_index_in_dim(halo_counts, here, axis=1, keepdims=False)
    live = jnp.arange(slots)[None, :] < arriving[:, None]
    projected = jnp.dot(hidden, neigh_l2, preferred_element_type=jnp.float32)
    block_proj = lax.all_gather(projected, "feat", axis=0, tiled=True)
    outgoing = jnp.take(block_proj, send_rows[0], axis=0)
    incoming = lax.all_to_all(outgoing, "node", split_axis=0, concat_axis=0, tiled=True)
    incoming = jnp.where(live[:, :, None], incoming, 0.0).reshape(-1, tile_size, classes)
    own_tiles = own_rows // tile_size
    first_tile = lax.axis_index("feat") * own_tiles
    my_tiles = lax.dynamic_slice_in_dim(intra_tiles, first_tile, own_tiles, 0)
    my_values = lax.dynamic_slice_in_dim(intra_values, first_tile, own_tiles, 0).astype(jnp.float32)
    my_cut_tiles = lax.dynamic_slice_in_dim(cut_tiles, first_tile, own_tiles, 0)
    my_cut_values = lax.dynamic_slice_in_dim(cut_values, first_tile, own_tiles, 0).astype(
        jnp.float32
    )
    inner = tile_sum(my_tiles, my_values, block_proj.reshape(row_tiles, tile_size, classes))
    outer = tile_sum(my_cut_tiles, my_cut_values, incoming)
    neighbour = (inner + outer).reshape(own_rows, classes)
    logits = jnp.dot(hidden, self_l2, preferred_element_type=jnp.float32) + neighbour
    return logits.astype(jnp.bfloat16)


def solution(mesh):
    placed = (
        P(("groups", "node"), "feat"),
        P(("groups", "node"), None),
        P(("groups", "node"), None, None, None),
        P(("groups", "node"), None),
        P(("groups", "node"), None, None, None),
        P(("groups", "node"), None, None),
        P("groups", None),
        P(),
        P(),
        P(),
        P(),
    )
    return jax.shard_map(
        shards,
        mesh=mesh,
        in_specs=placed,
        out_specs=P(("groups", "node", "feat"), None),
        check_vma=False,
    )
```

time: 121 us -> 107 us (0.88)
  local copies, waits for them, and re-layouts: 10.1 us -> 1.72 us
  other arithmetic: 2.51 us -> 0 us
  Pallas kernels: 107 us -> 105 us
    unnamed x9 -> x1, local copies, waits for them, and re-layouts: 8.18 us -> 1.72 us
    pallas_call x1, Pallas kernels: 107 us -> 105 us  [fused(): pl.pallas_call(kernel, out_shape=jax.ShapeDtypeStruct((classes, own_rows)...]
    pallas_call x1 -> x0, local copies, waits for them, and re-layouts: 1.95 us -> none  [fused(): pl.pallas_call(kernel, out_shape=jax.ShapeDtypeStruct((own_rows, classes)...]
    select_n x1 -> x0, other arithmetic: 1.35 us -> none  [fused(): jnp.where(jnp.arange(slots)[None, None, :] < leaving[None, :, None], send...]
where the time goes in v2:
time: 107 us
  Pallas kernels  105 us (98%)
  local copies, waits for them, and re-layouts  1.72 us (2%)
    pallas_call x1, Pallas kernels, fused(): pl.pallas_call(kernel, out_shape=jax.ShapeDtypeStruct((classes, own_rows)...  105 us

profile of v2, /device:TPU:1, one launch (start us, length us, event | category | flops | bytes accessed | tf_op | source)
XLA Modules:
  0.0 107.0 jit_solution(10315701754696364306)
XLA Ops:
  0.0 105.3 %shard_map.109 = bf16[153,1024]{1,0:T(8,128)(2,1)} custom-call(s32[3,32]{1,0:T(4,128)} %bitcast.14, s32[1,32]{1,0:T(1,128)} %bitcast.15, s32[1,4,256]{2,1,0:T(4,128)} %send_rows.1, s32[4,4]{1,0:T(4,128)} %counts.1, bf16[192,4096]{1,0:T(8,128)(2,1)} %bitcast.8, bf16[32,3,128,128]{3,2,1,0:T(8,128)(2,1)} %vals_h.1, bf16[32,1,128,128]{3,2,1,0:T(8,128)(2,1)} %cvals_h.1, ...), custom_call_target="tpu_custom_call" | custom-call | tf_op jit(solution)/shard_map/pallas_call | solution.py:282
  105.3 1.7 %copy.13 = bf16[1024,153]{0,1:T(8,128)(2,1)} copy(bf16[1024,153]{0,1:T(8,128)(2,1)} %bitcast.11) | data formatting | bytes 626688

commit v3 on v2

--- a/solution.py
+++ b/solution.py
@@ -7,6 +7,7 @@
 
 MESH = pl.DeviceIdType.MESH
 CHUNKS = 2
+PIECES = 2 * CHUNKS
 F32, BF16 = jnp.float32, jnp.bfloat16
 
 
@@ -26,6 +27,7 @@
     tiles, width, ts = feats.shape
     own_tiles = tiles // nz
     ct = own_tiles // CHUNKS
+    pt = own_tiles // PIECES
     part = ct * ts
     intra_k = vals.shape[1]
     slots = send_rows.shape[-1]
@@ -111,7 +113,7 @@
         lax.fori_loop(1, nz, step, 0)
 
     def ag_piece(source, c):
-        return gath.at[pl.ds(source * own_tiles + c * ct, ct)]
+        return gath.at[pl.ds(source * own_tiles + c * pt, pt)]
 
     def ag_copy(c, right, k):
         piece = ag_piece(z - k if right else z + k, c)
@@ -144,8 +146,8 @@
             ag_copy(c, False, k).wait_send()
 
     def flatten(source, c):
-        for i in range(ct):
-            t = source * own_tiles + c * ct + i
+        for i in range(pt):
+            t = source * own_tiles + c * pt + i
             rows = pl.ds(pl.multiple_of(t * ts, ts), ts)
             tile = gath[t].astype(F32)
             flat[rows, :128] = tile[:128].T
@@ -178,6 +180,9 @@
         def _():
             flatten(z + k, c)
 
+    def pieces(c):
+        return range(c * (PIECES // CHUNKS), (c + 1) * (PIECES // CHUNKS))
+
     proj[...] = jnp.zeros_like(proj)
     own[...] = jnp.zeros_like(own)
     flat[:, 128:] = jnp.zeros((flat.shape[0], 128), F32)
@@ -187,9 +192,11 @@
         proj[:classes, :] = dot(w2n[...], hidden, 1, 0)
         for i in range(ct):
             gath[z * own_tiles + c * ct + i] = proj[:, i * ts : (i + 1) * ts].astype(BF16)
-        ag_send(c, 0)
+        for p in pieces(c):
+            ag_send(p, 0)
         own[:classes, c * part : (c + 1) * part] = dot(w2s[...], hidden, 1, 0)
-        flatten(z, c)
+        for p in pieces(c):
+            flatten(z, p)
 
     for c in range(CHUNKS):
         start = pl.multiple_of((z * CHUNKS + c) * part, part)
@@ -197,14 +204,17 @@
         accumulate(1, z, agg[z, c])
         from_others(0, c)
         if c > 0:
-            ag_step(c - 1, 1)
+            for p in pieces(c - 1):
+                ag_step(p, 1)
         from_others(1, c)
         project(c)
         if c > 0:
             for k in range(2, nz):
-                ag_step(c - 1, k)
+                for p in pieces(c - 1):
+                    ag_step(p, k)
     for k in range(1, nz):
-        ag_step(CHUNKS - 1, k)
+        for p in pieces(CHUNKS - 1):
+            ag_step(p, k)
 
     def h_copy(off):
         return pltpu.make_async_remote_copy(
@@ -254,7 +264,8 @@
             for off in range(1, nz):
                 l1_copy(kind, off, c).wait_send()
         for k in range(nz - 1):
-            ag_sent(c, k)
+            for p in pieces(c):
+                ag_sent(p, k)
     for off in range(1, nn):
         h_copy(off).wait_send()
 
@@ -305,8 +316,8 @@
             dma((7,)),
             dma((2, nz - 1, CHUNKS)),
             dma((2, nz - 1, CHUNKS)),
-            dma((CHUNKS, 2, nz - 1)),
-            dma((CHUNKS, 2, nz - 1)),
+            dma((PIECES, 2, nz - 1)),
+            dma((PIECES, 2, nz - 1)),
             dma((nn - 1,)),
             dma((nn - 1,)),
         ],

time: 107 us -> 107 us (level)
  no operation moved by 1% of the time
where the time goes in v3:
time: 107 us
  Pallas kernels  105 us (98%)
  local copies, waits for them, and re-layouts  1.72 us (2%)
    pallas_call x1, Pallas kernels, fused(): pl.pallas_call(kernel, out_shape=jax.ShapeDtypeStruct((classes, own_rows)...  105 us

profile of v3, /device:TPU:1, one launch (start us, length us, event | category | flops | bytes accessed | tf_op | source)
XLA Modules:
  0.0 106.5 jit_solution(2478318961922070767)
XLA Ops:
  0.0 104.8 %shard_map.109 = bf16[153,1024]{1,0:T(8,128)(2,1)} custom-call(s32[3,32]{1,0:T(4,128)} %bitcast.14, s32[1,32]{1,0:T(1,128)} %bitcast.15, s32[1,4,256]{2,1,0:T(4,128)} %send_rows.1, s32[4,4]{1,0:T(4,128)} %counts.1, bf16[192,4096]{1,0:T(8,128)(2,1)} %bitcast.8, bf16[32,3,128,128]{3,2,1,0:T(8,128)(2,1)} %vals_h.1, bf16[32,1,128,128]{3,2,1,0:T(8,128)(2,1)} %cvals_h.1, ...), custom_call_target="tpu_custom_call" | custom-call | tf_op jit(solution)/shard_map/pallas_call | solution.py:293
  104.8 1.7 %copy.13 = bf16[1024,153]{0,1:T(8,128)(2,1)} copy(bf16[1024,153]{0,1:T(8,128)(2,1)} %bitcast.11) | data formatting | bytes 626688
